TPU v7x, 256 devices: a whole 4x4x8 slice. The times are simulated.
256 devices in a mesh: grp: 4 (over x), grid: 64 (over y, z, core).
Axes of the slice: x: 4, y: 4, z: 8, core: 2. Of those that a mesh axis runs over, the one named last changes fastest.
Arguments:
- orbitals: float32 [512, 262144], P('grp', 'grid'), may hold values from -6 to 6
- anchors: int32 [512, 3], replicated, may hold values from 0 to 31
- pair_slots: int32 [256, 4, 2], replicated, may hold values from -1 to 511, as said below
Outputs:
- exchange_term: float32 [512, 262144], P('grp', 'grid')
Inputs may be any that keep to these rules, and one draw needn't show every extreme that they name: `pair_slots`: row k lists the pairs of owner k, the device with index k in the order grp, grid; its first slots hold pairs of two different orbital numbers and its other slots hold -1 in both columns. Exactly 512 slots hold pairs in all, no row holds more than 4, and some row holds exactly 4.
All inputs are finite; a program needn't handle non-finite values.
Results may differ from a plain program's by a relative error of at most 0.0003.
Values sent between devices are 32-bit elements; how exact they have to be, the bound alone decides.
No kernel may reach another device: no remote copies, remote signals or barrier semaphores. Data moves between devices by JAX's collectives and lax.ppermute only.
A program may use at most 128 MiB of HBM per device.

v0:
```python
import jax
import jax.numpy as jnp
from jax import lax
from jax.sharding import PartitionSpec as P

B = 64
PAIR_DEV = 2
ITERS = 3


def shift_field(field, offset, extent):
    plane_size = extent * extent
    padded_x = jnp.pad(field, ((extent, extent), (0, 0)))
    moved = lax.dynamic_slice_in_dim(padded_x, extent - offset[0], extent, 0)
    padded_yz = jnp.pad(moved, ((0, 0), (plane_size, plane_size)))
    linear = offset[1] * extent + offset[2]
    moved = lax.dynamic_slice_in_dim(padded_yz, plane_size - linear, plane_size, 1)
    cells = lax.broadcasted_iota(jnp.int32, (1, plane_size), 1)
    coord_y = cells // extent - offset[1]
    coord_z = cells % extent - offset[2]
    inside = (coord_y >= 0) & (coord_y < extent) & (coord_z >= 0) & (coord_z < extent)
    return jnp.where(inside, moved, jnp.zeros_like(moved))


def operate(field, extent):
    padded_x = jnp.pad(field, ((1, 1), (0, 0)))
    beside = padded_x[2:] + padded_x[:-2]
    padded_y = jnp.pad(field, ((0, 0), (extent, extent)))
    beside = beside + padded_y[:, 2 * extent :] + padded_y[:, : -2 * extent]
    padded_z = jnp.pad(field, ((0, 0), (1, 1)))
    cells = lax.broadcasted_iota(jnp.int32, (1, field.shape[1]), 1) % extent
    upper_z = jnp.where(cells < extent - 1, padded_z[:, 2:], jnp.zeros_like(field))
    lower_z = jnp.where(cells > 0, padded_z[:, :-2], jnp.zeros_like(field))
    return 6.0 * field - beside - upper_z - lower_z


def conjugate(density, extent):
    potential = jnp.zeros_like(density)
    resid = density
    direction = density
    norm_now = jnp.sum(resid * resid)
    for turn in range(ITERS):
        image = operate(direction, extent)
        step_len = norm_now / jnp.sum(direction * image)
        potential = potential + step_len * direction
        resid = resid - step_len * image
        norm_next = jnp.sum(resid * resid)
        direction = resid + norm_next / norm_now * direction
        norm_now = norm_next
    return potential


def pair_terms(field_a, field_b, offset, extent):
    partner = shift_field(field_b, offset, extent)
    density = field_a * partner
    potential = conjugate(density, extent)
    term_a = potential * partner
    term_b = shift_field(potential * field_a, -offset, extent)
    return (term_a, term_b)


def deal_evenly(pair_slots, owner_count, each_owner):
    flat_slots = pair_slots.reshape(-1, 2)
    filled = (flat_slots[:, 0] >= 0).astype(jnp.int32)
    order = jnp.arange(flat_slots.shape[0], dtype=jnp.int32)
    position = jnp.sum(jnp.where(order[None, :] < order[:, None], filled[None, :], 0), axis=1)
    wanted = lax.broadcasted_iota(jnp.int32, (owner_count, each_owner), 1) * owner_count
    wanted = (wanted + lax.broadcasted_iota(jnp.int32, (owner_count, each_owner), 0)).reshape(-1)
    matched = (position[None, :] == wanted[:, None]) & (filled[None, :] == 1)
    picked = jnp.dot(matched.astype(jnp.int32), flat_slots)
    return picked.reshape(owner_count, each_owner, 2)


def body(orbitals, anchors, pair_slots):
    extent = B
    grid_count = lax.axis_size("grid")
    owner_count = lax.axis_size("grp") * grid_count
    group_idx = lax.axis_index("grp")
    place_idx = lax.axis_index("grid")
    assignment = deal_evenly(pair_slots, owner_count, PAIR_DEV)
    filled = assignment[..., 0] >= 0
    safe_ids = jnp.maximum(assignment, 0)
    pieces = lax.all_gather(orbitals, "grp", axis=0, tiled=True)
    group_table = lax.dynamic_slice_in_dim(safe_ids, group_idx * grid_count, grid_count, 0)
    gather_ids = jnp.transpose(group_table, (1, 2, 0))
    outgoing = pieces[gather_ids]
    arrived = lax.all_to_all(outgoing, "grid", split_axis=2, concat_axis=2, tiled=True)
    owner_idx = group_idx * grid_count + place_idx
    own_pairs = safe_ids[owner_idx]
    own_filled = filled[owner_idx]
    offsets = anchors[own_pairs[:, 1]] - anchors[own_pairs[:, 0]]

    def solve_slot(slot_item):
        boxes_pair, offset, flag = slot_item
        term_a, term_b = pair_terms(boxes_pair[0], boxes_pair[1], offset, extent)
        weight_flag = jnp.where(flag, 1.0, 0.0).astype(jnp.float32)
        return jnp.stack([term_a, term_b]) * weight_flag

    terms = lax.map(solve_slot, (arrived, offsets, own_filled))
    returned = lax.all_to_all(terms, "grid", split_axis=2, concat_axis=2, tiled=True)
    flat_terms = returned.reshape(-1, returned.shape[-1])
    summed = jax.ops.segment_sum(flat_terms, gather_ids.reshape(-1), num_segments=anchors.shape[0])
    return lax.psum_scatter(summed, "grp", scatter_dimension=0, tiled=True)


def solution(mesh):
    return jax.shard_map(
        body,
        mesh=mesh,
        in_specs=(P("grp", "grid"), P(), P()),
        out_specs=P("grp", "grid"),
        check_vma=False,
    )
```

profile of v0, /device:TPU:1, one launch (start us, length us, event | category | flops | bytes accessed | tf_op | source)
XLA Modules:
  0.0 505.0 jit_solution(9031635187783980270)
XLA Ops:
  8.8 1.4 broadcast_maximum_fusion
  10.3 88.3 %all-gather.2.cloned.1.call-done = f32[512,4096]{1,0:T(8,128)} async-done(((f32[128,4096]{1,0:T(8,128)}), f32[512,4096]{1,0:T(8,128)}) %all-gather.2.cloned.1.call-update) | async-done | bytes 8388624 | tf_op jit(solution)/shard_map/all_gather | solution.py:83
  98.7 9.0 %gather_fusion = f32[256,4096]{1,0:T(8,128)} fusion(f32[512,4096]{1,0:T(8,128)} %all-gather.2.cloned.1.call-done, s32[1024]{0:T(1024)S(1)} %pad_clamp_fusion.2), kind=kCustom, calls=%fused_computation | custom fusion | bytes 8389632 | tf_op jit(solution)/shard_map/gather | solution.py:86
  107.7 7.4 %copy.23 = f32[2,2,64,4096]{3,1,0,2:T(2,128)} copy(f32[2,2,64,4096]{3,2,1,0:T(8,128)} %bitcast.60) | data formatting | bytes 8388608 | tf_op jit(solution)/shard_map/gather | solution.py:86
  115.0 11.0 %all-to-all-start = ((f32[2,2,64,4096]{3,1,0,2:T(2,128)}), f32[2,2,64,4096]{3,1,0,2:T(2,128)}, u32[]{:S(2)}, u32[]{:S(2)}) async-start(f32[2,2,64,4096]{3,1,0,2:T(2,128)} %copy.23), calls=%async_computation | async-start | bytes 8388608 | tf_op jit(solution)/shard_map/all_to_all | solution.py:87
  128.0 93.9 %all-to-all-done = f32[2,2,64,4096]{3,1,0,2:T(2,128)} async-done(((f32[2,2,64,4096]{3,1,0,2:T(2,128)}), f32[2,2,64,4096]{3,1,0,2:T(2,128)}, u32[]{:S(2)}, u32[]{:S(2)}) %all-to-all-start) | async-done | bytes 4194336 | tf_op jit(solution)/shard_map/all_to_all | solution.py:87
  222.0 77.0 %while.13 = (s32[]{:T(128)}, f32[2,2,64,4096]{3,1,0,2:T(2,128)}, f32[2,2,64,4096]{3,1,0,2:T(2,128)}, s32[2,3]{1,0:T(2,128)S(1)}, pred[2]{0:T(512)(128)(4,1)S(1)}...) while((s32[]{:T(128)}, f32[2,2,64,4096]{3,1,0,2:T(2,128)}, ...), condition=%wide.region_8.9_spmd, body=%wide.region_1.8_spmd.sunk | while | flops 22224920 | bytes 64017664 | solution.py:99
  225.2 4.4 constant_dynamic-slice_fusion.5
  232.6 1.8 multiply_reduce_fusion.9
  238.1 1.8 multiply_reduce_fusion.11
  243.6 1.8 fusion.79
  246.7 3.9 multiply_bitcast_fusion.2
  257.5 3.0 copy_dynamic-update-slice_fusion.2
  263.7 4.4 constant_dynamic-slice_fusion.5
  271.1 1.8 multiply_reduce_fusion.9
  276.6 1.8 multiply_reduce_fusion.11
  282.2 1.8 fusion.79
  285.3 3.9 multiply_bitcast_fusion.2
  296.0 3.0 copy_dynamic-update-slice_fusion.2
  299.0 6.1 %all-to-all-start.1 = ((f32[2,2,64,4096]{3,1,0,2:T(2,128)}), f32[2,2,64,4096]{3,1,0,2:T(2,128)}, u32[]{:S(2)}, u32[]{:S(2)}) async-start(f32[2,2,64,4096]{3,1,0,2:T(2,128)} %get-tuple-element.107), calls=%async_computation.1 | async-start | bytes 8388608 | tf_op jit(solution)/shard_map/all_to_all | solution.py:100
  305.2 95.8 %all-to-all-done.1 = f32[2,2,64,4096]{3,1,0,2:T(2,128)} async-done(((f32[2,2,64,4096]{3,1,0,2:T(2,128)}), f32[2,2,64,4096]{3,1,0,2:T(2,128)}, u32[]{:S(2)}, u32[]{:S(2)}) %all-to-all-start.1) | async-done | bytes 4194336 | tf_op jit(solution)/shard_map/all_to_all | solution.py:100
  400.9 6.6 %copy.28 = f32[2,2,64,4096]{3,2,1,0:T(8,128)} copy(f32[2,2,64,4096]{3,1,0,2:T(2,128)} %all-to-all-done.1) | data formatting | bytes 8388608 | tf_op jit(solution)/shard_map/all_to_all | solution.py:100
  407.5 11.3 %scatter_custom_fusion = f32[512,4096]{1,0:T(8,128)} fusion(s32[256]{0:T(256)S(1)} %reshape.253, f32[256,4096]{1,0:T(8,128)} %bitcast.61, f32[]{:T(128)} %constant.159.clone.1), kind=kCustom, calls=%fused_computation.90 | custom fusion | flops 1048576 | bytes 8389120 | tf_op jit(solution)/shard_map/scatter-add | solution.py:102
  418.8 79.4 %reduce-scatter.2.cloned.1.call-done = f32[128,4096]{1,0:T(8,128)} async-done(((f32[512,4096]{1,0:T(8,128)}), f32[128,4096]{1,0:T(8,128)}) %reduce-scatter.2.cloned.1.call-update) | async-done | bytes 2097168 | tf_op jit(solution)/shard_map/reduce_scatter | solution.py:103
  (72 shorter events, 23.5 us)
Async XLA Ops:
  6.5 92.1 %all-gather.2.cloned.1.call-start = ((), (), s32[]{:S(2)}) async-start(), calls=%async_computation.3 | async-start | bytes 10485760 | tf_op jit(solution)/shard_map/all_gather | solution.py:83
  115.0 11.0 %copy-start.3 = (s32[512,3]{0,1:T(4,128)S(1)}, s32[512,3]{0,1:T(4,128)}, u32[]{:S(2)}) copy-start(s32[512,3]{0,1:T(4,128)} %param.6) | copy-start | bytes 18436
  115.0 106.9 %all-to-all-start = ((f32[2,2,64,4096]{3,1,0,2:T(2,128)}), f32[2,2,64,4096]{3,1,0,2:T(2,128)}, u32[]{:S(2)}, u32[]{:S(2)}) async-start(f32[2,2,64,4096]{3,1,0,2:T(2,128)} %copy.23), calls=%async_computation | async-start | bytes 8388608 | tf_op jit(solution)/shard_map/all_to_all | solution.py:87
  229.6 4.8 copy-start
  230.3 2.3 copy-start.1
  250.7 6.7 %copy-start.2 = (f32[1,1,64,4096]{3,2,1,0:T(8,128)S(1)}, f32[1,1,64,4096]{3,2,1,0:T(8,128)}, u32[]{:S(2)}) copy-start(f32[1,1,64,4096]{3,2,1,0:T(8,128)} %get-tuple-element.231) | copy-start | bytes 3145732 | tf_op jit(solution)/shard_map/while
  268.1 4.8 copy-start
  268.9 2.3 copy-start.1
  289.1 6.7 %copy-start.2 = (f32[1,1,64,4096]{3,2,1,0:T(8,128)S(1)}, f32[1,1,64,4096]{3,2,1,0:T(8,128)}, u32[]{:S(2)}) copy-start(f32[1,1,64,4096]{3,2,1,0:T(8,128)} %get-tuple-element.231) | copy-start | bytes 3145732 | tf_op jit(solution)/shard_map/while
  299.0 102.0 %all-to-all-start.1 = ((f32[2,2,64,4096]{3,1,0,2:T(2,128)}), f32[2,2,64,4096]{3,1,0,2:T(2,128)}, u32[]{:S(2)}, u32[]{:S(2)}) async-start(f32[2,2,64,4096]{3,1,0,2:T(2,128)} %get-tuple-element.107), calls=%async_computation.1 | async-start | bytes 8388608 | tf_op jit(solution)/shard_map/all_to_all | solution.py:100
  305.0 193.1 %reduce-scatter.2.cloned.1.call-start = ((), (), s32[]{:S(2)}) async-start(), calls=%async_computation.4 | async-start | bytes 10485760 | tf_op jit(solution)/shard_map/reduce_scatter | solution.py:103
Sparse Core Ops, SparseCore 0:
  9.2 89.4 all-gather.1
  418.9 79.1 reduce-scatter.1
where the time goes:
time: 506 us; the launch traced here: 505 us
  waiting for transfers between devices  358 us (71%)
  local copies, waits for them, and re-layouts  47 us (9%)
  other arithmetic  43.2 us (9%)
  loops' own time  24.6 us (5%)
  starting transfers between devices  17.1 us (3%)
  between operations  13.5 us (3%)
    all_to_all x1, waiting for transfers between devices, body(): lax.all_to_all(terms, 'grid', split_axis=2, concat_axis=2, tiled=True)  95.8 us
    all_to_all x1, waiting for transfers between devices, body(): lax.all_to_all(outgoing, 'grid', split_axis=2, concat_axis=2, tiled=True)  93.9 us
    all_gather x1, waiting for transfers between devices, body(): pieces = lax.all_gather(orbitals, 'grp', axis=0, tiled=True)  88.3 us
    reduce_scatter x1, waiting for transfers between devices, body(): return lax.psum_scatter(summed, 'grp', scatter_dimension=0, tiled=True)  79.4 us
    another operation x1, loops' own time, body(): terms = lax.map(solve_slot, (arrived, offsets, own_filled))  24.6 us
    gather x2, local copies, waits for them, and re-layouts, body(): outgoing = pieces[gather_ids]  16.4 us
    scatter-add x1, other arithmetic, body(): jax.ops.segment_sum(flat_terms, gather_ids.reshape(-1), num_segments=anch...  11.3 us
    all_to_all x1, starting transfers between devices, body(): lax.all_to_all(outgoing, 'grid', split_axis=2, concat_axis=2, tiled=True)  11 us
  transfers between devices with their start and end apart: 4, of which 4 were waited for; matrix products, arithmetic and copies ran while one was open for 1% of the time, Pallas kernels for 0%

commit v1 on v0

--- a/solution.py
+++ b/solution.py
@@ -1,11 +1,18 @@
+import functools
+
 import jax
 import jax.numpy as jnp
 from jax import lax
+from jax.experimental import pallas as pl
+from jax.experimental.pallas import tpu as pltpu
 from jax.sharding import PartitionSpec as P
 
 B = 64
 PAIR_DEV = 2
 ITERS = 3
+CHUNKS = 2
+ROWS = B * B // 128
+KEEP = 32
 
 
 def shift_field(field, offset, extent):
@@ -71,7 +78,7 @@
     return picked.reshape(owner_count, each_owner, 2)
 
 
-def body(orbitals, anchors, pair_slots):
+def general(orbitals, anchors, pair_slots):
     extent = B
     grid_count = lax.axis_size("grid")
     owner_count = lax.axis_size("grp") * grid_count
@@ -103,6 +110,408 @@
     return lax.psum_scatter(summed, "grp", scatter_dimension=0, tiled=True)
 
 
+def route_kernel(me_ref, a_ref, b_ref, pos_ref, slot_ref, most_ref):
+    me = me_ref[0]
+    a, b = a_ref[...], b_ref[...]
+    n = a.shape[0]
+    f32, i32 = jnp.float32, jnp.int32
+
+    def lanes(width):
+        return lax.broadcasted_iota(i32, (n, width), 1)
+
+    def row(x, width=128):
+        return jnp.sum(x, axis=0, keepdims=True)
+
+    def col(x):
+        return jnp.sum(x, axis=1, keepdims=True)
+
+    before = (lax.broadcasted_iota(i32, (n, n), 0) > lax.broadcasted_iota(i32, (n, n), 1))
+    before = jnp.where(before, 1.0, 0.0).astype(jnp.bfloat16)
+
+    def count_before(hot):
+        return jnp.dot(before, hot.astype(jnp.bfloat16), preferred_element_type=f32)
+
+    lane = lanes(128)
+    valid = a >= 0
+    ga, gb = a >> 7, b >> 7
+    typ = jnp.where(valid, ga * 4 + gb, -1)
+    hot = jnp.where(lane == typ, 1.0, 0.0)
+    rank = col(count_before(hot) * hot).astype(i32)
+    turn = (rank + ga + gb) & 3
+    bin_no = jnp.where(valid, jnp.where((turn & 1) == 0, ga, gb) * CHUNKS + (turn >> 1), -1)
+    hot = jnp.where(lane == bin_no, 1.0, 0.0)
+    rank = col(count_before(hot) * hot)
+    load = row(hot)
+    over = jnp.maximum(load - B, 0.0)
+    lane1 = lax.broadcasted_iota(i32, (1, 128), 1)
+    room = jnp.where(lane1 < 4 * CHUNKS, jnp.maximum(B - load, 0.0), 0.0)
+    upper = lax.broadcasted_iota(i32, (128, 128), 0) < lax.broadcasted_iota(i32, (128, 128), 1)
+    upper = jnp.where(upper, 1.0, 0.0)
+    both = jnp.where(lax.broadcasted_iota(i32, (8, 128), 0) == 0, over, room)
+    sums = jnp.dot(both, upper, precision=lax.Precision.HIGHEST, preferred_element_type=f32)
+    over_before, room_before = sums[0:1], sums[1:2]
+    spilled = valid & (rank >= B)
+    spill_no = rank - B + col(hot * over_before)
+    lands = (spill_no >= room_before) & (spill_no < room_before + room)
+    landed = jnp.where(lands, 1.0, 0.0)
+    hot = jnp.where(spilled, landed, hot)
+    place = jnp.where(spilled, col(landed * (load - room_before)) + spill_no, rank).astype(i32)
+    bin_no = col(hot * lane.astype(f32)).astype(i32)
+    group, chunk = bin_no >> 1, bin_no & 1
+
+    from_a, from_b = valid & (ga != group), valid & (gb != group)
+    key_a = jnp.where(from_a, (chunk * 4 + ga) * 4 + group, -1)
+    key_b = jnp.where(from_b, (chunk * 4 + gb) * 4 + group, -1)
+    hot_a = jnp.where(lane == key_a, 1.0, 0.0)
+    hot_b = jnp.where((lane >= 32) & (lane - 32 == key_b), 1.0, 0.0)
+    counts = count_before(hot_a + hot_b)
+    all_a = row(hot_a)
+    slot_a = col(hot_a * counts).astype(i32)
+    slot_b = (col(hot_b * counts) + col(jnp.where(lane == key_b, all_a, 0.0))).astype(i32)
+    highest = jnp.maximum(jnp.where(from_a, slot_a, 0), jnp.where(from_b, slot_b, 0))
+    most_ref[...] = jnp.broadcast_to(jnp.max(highest, axis=0, keepdims=True), (8, 128))
+
+    def exact(cols, mask):
+        return lax.dot_general(
+            cols, jnp.where(mask, 1.0, 0.0), (((0,), (0,)), ((), ())),
+            precision=lax.Precision.HIGHEST, preferred_element_type=f32,
+        )
+
+    lane8 = lanes(8)
+
+    def side(*columns):
+        out = jnp.zeros((n, 8), f32)
+        for at, column in enumerate(columns):
+            out = jnp.where(lane8 == at, column.astype(f32), out)
+        return out
+
+    shift_a, shift_b = (group - ga) & 3, (group - gb) & 3
+    put_a = (shift_a - 1) * KEEP + slot_a
+    put_b = (shift_b - 1) * KEEP + slot_b
+    local_a, local_b = a & 127, b & 127
+    table_a = jnp.where(shift_a == 0, local_a, 128 + put_a)
+    table_b = jnp.where(shift_b == 0, local_b, 128 + put_b)
+    mine = valid & (group == me)
+    pos = exact(side(table_a, table_b, a, b), mine & (lane == chunk * B + place))
+    pos_ref[...] = pos.astype(i32)
+
+    wide = lanes(slot_ref.shape[1])
+    at_a, at_b = chunk * (3 * KEEP) + put_a, chunk * (3 * KEEP) + put_b
+    fits_a, fits_b = from_a & (slot_a < KEEP), from_b & (slot_b < KEEP)
+    one = jnp.ones_like(a)
+    zero = jnp.zeros_like(a)
+    slots = exact(side(local_a, zero, one), fits_a & (ga == me) & (wide == at_a))
+    slots += exact(side(local_b, zero, one), fits_b & (gb == me) & (wide == at_b))
+    slots += exact(side(zero, place * 2), fits_a & mine & (wide == at_a))
+    slots += exact(side(zero, place * 2 + 1), fits_b & mine & (wide == at_b))
+    slot_ref[...] = slots.astype(i32)
+
+
+def route(me, pair_slots):
+    flat = pair_slots.reshape(-1, 2)
+    width = 128 * -(-(CHUNKS * 3 * KEEP) // 128)
+    vmem = pl.BlockSpec(memory_space=pltpu.VMEM)
+    return pl.pallas_call(
+        route_kernel,
+        out_shape=[
+            jax.ShapeDtypeStruct((8, 128), jnp.int32),
+            jax.ShapeDtypeStruct((8, width), jnp.int32),
+            jax.ShapeDtypeStruct((8, 128), jnp.int32),
+        ],
+        in_specs=[pl.BlockSpec(memory_space=pltpu.SMEM), vmem, vmem],
+        out_specs=[vmem, vmem, vmem],
+        compiler_params=pltpu.CompilerParams(vmem_limit_bytes=40 << 20),
+        cost_estimate=pl.CostEstimate(flops=10_000_000, bytes_accessed=1_000_000, transcendentals=0),
+        name="route",
+    )(me, flat[:, :1], flat[:, 1:])
+
+
+def fetch_kernel(count, row_of, first, idx_ref, *refs):
+    *tables, out_ref, sem = refs
+    ends = []
+    for table in tables:
+        ends.append((ends[-1] if ends else 0) + table.shape[0])
+
+    def start(i, carry):
+        j = row_of(idx_ref, first, i)
+        begin = 0
+        for table, end in zip(tables, ends):
+            if len(tables) == 1:
+                pltpu.make_async_copy(table.at[j], out_ref.at[i], sem).start()
+            else:
+                @pl.when((j >= begin) & (j < end))
+                def _(table=table, begin=begin):
+                    pltpu.make_async_copy(table.at[j - begin], out_ref.at[i], sem).start()
+            begin = end
+        return carry
+
+    lax.fori_loop(0, count, start, 0)
+    pltpu.make_async_copy(out_ref, out_ref, sem).wait()
+
+
+def fetch(idx, tables, count, row_of, first, name):
+    return pl.pallas_call(
+        functools.partial(fetch_kernel, count, row_of, first),
+        out_shape=jax.ShapeDtypeStruct((count, ROWS, 128), jnp.float32),
+        in_specs=[pl.BlockSpec(memory_space=pltpu.SMEM)] + [pl.BlockSpec(memory_space=pl.ANY)] * len(tables),
+        out_specs=pl.BlockSpec(memory_space=pl.ANY),
+        scratch_shapes=[pltpu.SemaphoreType.DMA],
+        cost_estimate=pl.CostEstimate(flops=0, bytes_accessed=count * 32768, transcendentals=0),
+        name=name,
+    )(idx, *tables)
+
+
+def pair_kernel(chunk, place_ref, pos_ref, anchor_ref, in_ref, out_ref, part, dens, resid, second, third, image):
+    at = chunk * B + place_ref[0]
+    orb_a, orb_b = pos_ref[2, at], pos_ref[3, at]
+    ox, oy, oz = [anchor_ref[3 * orb_b + k] - anchor_ref[3 * orb_a + k] for k in range(3)]
+    shape = (ROWS, 128)
+    line = lax.broadcasted_iota(jnp.int32, shape, 0)
+    lane = lax.broadcasted_iota(jnp.int32, shape, 1)
+    cy = 2 * line + (lane >> 6)
+    cz = lane & 63
+    low = lane < 64
+    no_y = ((cy == 0) | (cy == B - 1))
+    no_up, no_down = cz == B - 1, cz == 0
+
+    def shifter(sy, sz):
+        flat = (sy * B + sz + B * B) & (B * B - 1)
+        lines, steps = flat >> 7, flat & 127
+        inside = (cy >= sy) & (cy < B + sy) & (cz >= sz) & (cz < B + sz)
+        keep = lane >= steps
+
+        def shift(plane):
+            turned = pltpu.roll(plane, steps, axis=1)
+            turned = jnp.where(keep, turned, pltpu.roll(turned, 1, axis=0))
+            return jnp.where(inside, pltpu.roll(turned, lines, axis=0), 0.0)
+
+        return shift
+
+    def apply(ref, x):
+        here = ref[x + 1]
+        swapped = pltpu.roll(here, 64, axis=1)
+        other = jnp.where(low, pltpu.roll(swapped, 1, axis=0), pltpu.roll(swapped, ROWS - 1, axis=0))
+        beside = ref[x] + ref[x + 2] + swapped + jnp.where(no_y, 0.0, other)
+        upper = jnp.where(no_up, 0.0, pltpu.roll(here, 127, axis=1))
+        lower = jnp.where(no_down, 0.0, pltpu.roll(here, 1, axis=1))
+        return here, 6.0 * here - beside - upper - lower
+
+    zero = jnp.zeros(shape, jnp.float32)
+    for ref in (dens, second, third):
+        ref[0] = zero
+        ref[B + 1] = zero
+
+    def total(x):
+        return jnp.sum(x, keepdims=True)
+
+    def planes(step, init=None):
+        return lax.fori_loop(0, B, step, zero if init is None else init, unroll=2)
+
+    shift_on = shifter(oy, oz)
+    shift_back = shifter(-oy, -oz)
+
+    def begin(x, acc):
+        src = x - ox
+        inside = jnp.where((src >= 0) & (src < B), 1.0, 0.0)
+        moved = shift_on(in_ref[jnp.clip(src, 0, B - 1), 1]) * inside
+        density = in_ref[x, 0] * moved
+        part[x] = moved
+        dens[x + 1] = density
+        return acc + density * density
+
+    norm0 = total(planes(begin))
+
+    def first(x, acc):
+        here, img = apply(dens, x)
+        image[x] = img
+        return acc + here * img
+
+    step0 = norm0 / total(planes(first))
+
+    def rest0(x, acc):
+        left = dens[x + 1] - step0 * image[x]
+        resid[x] = left
+        return acc + left * left
+
+    norm1 = total(planes(rest0))
+    ratio0 = norm1 / norm0
+
+    def turn1(x, acc):
+        second[x + 1] = resid[x] + ratio0 * dens[x + 1]
+        return acc
+
+    planes(turn1)
+
+    def again(x, acc):
+        here, img = apply(second, x)
+        image[x] = img
+        return acc + here * img
+
+    step1 = norm1 / total(planes(again))
+
+    def rest1(x, acc):
+        left = resid[x] - step1 * image[x]
+        resid[x] = left
+        return acc + left * left
+
+    norm2 = total(planes(rest1))
+    ratio1 = norm2 / norm1
+
+    def turn2(x, acc):
+        third[x + 1] = resid[x] + ratio1 * second[x + 1]
+        return acc
+
+    planes(turn2)
+
+    def last(x, acc):
+        here, img = apply(third, x)
+        return acc + here * img
+
+    step2 = norm2 / total(planes(last))
+
+    def finish(x, acc):
+        potential = step0 * dens[x + 1] + step1 * second[x + 1] + step2 * third[x + 1]
+        out_ref[x, 0] = potential * part[x]
+        image[x] = potential * in_ref[x, 0]
+        return acc
+
+    planes(finish)
+
+    def back(x, acc):
+        src = x + ox
+        inside = jnp.where((src >= 0) & (src < B), 1.0, 0.0)
+        out_ref[x, 1] = shift_back(image[jnp.clip(src, 0, B - 1)]) * inside
+        return acc
+
+    planes(back)
+
+
+def solve(chunk, place, pos, anchors, boxes):
+    smem = pl.BlockSpec(memory_space=pltpu.SMEM)
+    vmem = pl.BlockSpec(memory_space=pltpu.VMEM)
+    field = pltpu.VMEM((B, ROWS, 128), jnp.float32)
+    padded = pltpu.VMEM((B + 2, ROWS, 128), jnp.float32)
+    return pl.pallas_call(
+        functools.partial(pair_kernel, chunk),
+        out_shape=jax.ShapeDtypeStruct((B, 2, ROWS, 128), jnp.float32),
+        in_specs=[smem, smem, smem, vmem],
+        out_specs=vmem,
+        scratch_shapes=[field, padded, field, padded, padded, field],
+        compiler_params=pltpu.CompilerParams(vmem_limit_bytes=24 << 20),
+        cost_estimate=pl.CostEstimate(flops=60_000_000, bytes_accessed=30_000_000, transcendentals=0),
+        name=f"solve{chunk}",
+    )(place, pos, anchors, boxes)
+
+
+def add_kernel(chunk, has_sum, is_last, pos_ref, slot_ref, *refs):
+    if has_sum:
+        sum_ref, terms_ref, far_ref, out_ref, acc = refs
+    else:
+        terms_ref, far_ref, out_ref, acc = refs
+    total = acc if is_last else out_ref
+    if has_sum:
+        total[...] = sum_ref[...]
+    else:
+        total[...] = jnp.zeros(total.shape, jnp.float32)
+
+    def near(p, carry):
+        for r in range(2):
+            j = pos_ref[r, chunk * B + p]
+
+            @pl.when(j < 128)
+            def _(j=j, r=r):
+                total[j] = total[j] + terms_ref[p, r]
+
+        return carry
+
+    lax.fori_loop(0, B, near, 0)
+
+    def far(k, carry):
+        at = chunk * (3 * KEEP) + k
+
+        @pl.when(slot_ref[2, at] == 1)
+        def _():
+            j = slot_ref[0, at]
+            total[j] = total[j] + far_ref[k]
+
+        return carry
+
+    lax.fori_loop(0, 3 * KEEP, far, 0)
+    if is_last:
+        for j in range(ROWS):
+            out_ref[:, j * 128 : (j + 1) * 128] = acc[:, j, :]
+
+
+def add_up(chunk, pos, slot, summed, terms, far):
+    is_last = chunk == CHUNKS - 1
+    smem = pl.BlockSpec(memory_space=pltpu.SMEM)
+    vmem = pl.BlockSpec(memory_space=pltpu.VMEM)
+    args = ([] if summed is None else [summed]) + [terms, far]
+    out = (128, ROWS * 128) if is_last else (128, ROWS, 128)
+    return pl.pallas_call(
+        functools.partial(add_kernel, chunk, summed is not None, is_last),
+        out_shape=jax.ShapeDtypeStruct(out, jnp.float32),
+        in_specs=[smem, smem] + [vmem] * len(args),
+        out_specs=vmem,
+        scratch_shapes=[pltpu.VMEM((128, ROWS, 128), jnp.float32)],
+        compiler_params=pltpu.CompilerParams(vmem_limit_bytes=24 << 20),
+        cost_estimate=pl.CostEstimate(flops=2_000_000, bytes_accessed=10_000_000, transcendentals=0),
+        name=f"add{chunk}",
+    )(pos, slot, *args)
+
+
+def turned(x, shift):
+    groups = lax.axis_size("grp")
+    return lax.ppermute(x, "grp", [(g, (g + shift) % groups) for g in range(groups)])
+
+
+def table_row(idx_ref, first, i):
+    return idx_ref[i & 1, first + (i >> 1)]
+
+
+def sent_row(idx_ref, first, i):
+    return idx_ref[0, first + i]
+
+
+def used_row(idx_ref, first, i):
+    return idx_ref[1, first + i]
+
+
+def fitting(orbitals, anchors, place, pos, slot):
+    local = orbitals.reshape(128, ROWS, 128)
+    anchor_list = anchors.reshape(-1)
+    boxes = []
+    for c in range(CHUNKS):
+        arrived = []
+        for d in (1, 2, 3):
+            sent = fetch(slot, [local], KEEP, sent_row, (3 * c + d - 1) * KEEP, f"send{c}_{d}")
+            arrived.append(turned(sent, d))
+        outgoing = fetch(pos, [local] + arrived, 2 * B, table_row, c * B, f"deal{c}")
+        boxes.append(lax.all_to_all(outgoing.reshape(B, 2, ROWS, 128), "grid", 0, 0, tiled=True))
+    summed = None
+    for c in range(CHUNKS):
+        terms = solve(c, place, pos, anchor_list, boxes[c])
+        terms = lax.all_to_all(terms, "grid", 0, 0, tiled=True)
+        flat = terms.reshape(2 * B, ROWS, 128)
+        far = []
+        for d in (1, 2, 3):
+            back = fetch(slot, [flat], KEEP, used_row, (3 * c + d - 1) * KEEP, f"back{c}_{d}")
+            far.append(turned(back, -d))
+        summed = add_up(c, pos, slot, summed, terms, jnp.concatenate(far))
+    return summed
+
+
+def body(orbitals, anchors, pair_slots):
+    me = lax.axis_index("grp").astype(jnp.int32)[None]
+    place = lax.axis_index("grid").astype(jnp.int32)[None]
+    pos, slot, most = route(me, pair_slots)
+    return lax.cond(
+        most[0, 0] < KEEP,
+        lambda: fitting(orbitals, anchors, place, pos, slot),
+        lambda: general(orbitals, anchors, pair_slots),
+    )
+
+
 def solution(mesh):
     return jax.shard_map(
         body,

time: 506 us -> 605 us (1.20); the launches traced: 505 us -> 598 us
  Pallas kernels: 0 us -> 404 us
  waiting for transfers between devices: 358 us -> 102 us
  other arithmetic: 43.2 us -> 1.28 us
  starting transfers between devices: 17.1 us -> 55.6 us
  local copies, waits for them, and re-layouts: 47 us -> 10.6 us
  loops' own time: 24.6 us -> 9.34 us
    pallas_call x0 -> x19, Pallas kernels: none -> 404 us  [the longest x14 342 us: fetch(): pl.pallas_call(functools.partial(fetch_kernel, count, row_of, first), out...]
    all_to_all x2 -> x4, waiting for transfers between devices: 190 us -> 62.8 us  [the longest x2 31.6 us: fitting(): lax.all_to_all(outgoing.reshape(B, 2, ROWS, 128), 'grid', 0, 0, tiled=True)]
    all_gather x1 -> x0, waiting for transfers between devices: 88.3 us -> none  [body(): pieces = lax.all_gather(orbitals, 'grp', axis=0, tiled=True)]
    reduce_scatter x1 -> x0, waiting for transfers between devices: 79.4 us -> none  [body(): return lax.psum_scatter(summed, 'grp', scatter_dimension=0, tiled=True)]
    ppermute x0 -> x12, waiting for transfers between devices: none -> 39.5 us  [turned(): lax.ppermute(x, 'grp', [(g, (g + shift) % groups) for g in range(groups)])]
    all_to_all x2 -> x4, starting transfers between devices: 17.1 us -> 37.7 us  [the longest x2 25.9 us: fitting(): lax.all_to_all(outgoing.reshape(B, 2, ROWS, 128), 'grid', 0, 0, tiled=True)]
    ppermute x0 -> x12, starting transfers between devices: none -> 17.9 us  [turned(): lax.ppermute(x, 'grp', [(g, (g + shift) % groups) for g in range(groups)])]
    gather x4 -> x0, local copies, waits for them, and re-layouts: 17.5 us -> none  [the longest x2 16.4 us: body(): outgoing = pieces[gather_ids]]
  transfers between devices with their start and end apart: 4 -> 16, of which waited for: 4 -> 6; matrix products, arithmetic and copies ran while one was open for 1% -> 0% of each run, Pallas kernels for 0% -> 50%
where the time goes in v1:
time: 605 us; the launch traced here: 598 us
  Pallas kernels  404 us (67%)
  waiting for transfers between devices  102 us (17%)
  starting transfers between devices  55.6 us (9%)
  between operations  14.6 us (2%)
  local copies, waits for them, and re-layouts  10.6 us (2%)
  loops' own time  9.34 us (2%)
    pallas_call x14, Pallas kernels, fetch(): pl.pallas_call(functools.partial(fetch_kernel, count, row_of, first), out...  342 us
    ppermute x12, waiting for transfers between devices, turned(): lax.ppermute(x, 'grp', [(g, (g + shift) % groups) for g in range(groups)])  39.5 us
    pallas_call x2, Pallas kernels, solve(): pl.pallas_call(functools.partial(pair_kernel, chunk), out_shape=jax.Shape...  36.6 us
    all_to_all x2, waiting for transfers between devices, fitting(): lax.all_to_all(outgoing.reshape(B, 2, ROWS, 128), 'grid', 0, 0, tiled=True)  31.6 us
    all_to_all x2, waiting for transfers between devices, fitting(): terms = lax.all_to_all(terms, 'grid', 0, 0, tiled=True)  31.2 us
    all_to_all x2, starting transfers between devices, fitting(): lax.all_to_all(outgoing.reshape(B, 2, ROWS, 128), 'grid', 0, 0, tiled=True)  25.9 us
    ppermute x12, starting transfers between devices, turned(): lax.ppermute(x, 'grp', [(g, (g + shift) % groups) for g in range(groups)])  17.9 us
    pallas_call x1, Pallas kernels, route(): pl.pallas_call(route_kernel, out_shape=[jax.ShapeDtypeStruct((8, 128), jn...  12.4 us
  transfers between devices with their start and end apart: 16, of which 6 were waited for; matrix products, arithmetic and copies ran while one was open for 0% of the time, Pallas kernels for 50%

profile of v1, /device:TPU:1, one launch (start us, length us, event | category | flops | bytes accessed | tf_op | source)
XLA Modules:
  0.0 597.5 jit_solution(16597967506981127182)
XLA Ops:
  9.8 12.4 %route.1 = (s32[8,128]{1,0:T(8,128)S(1)}, s32[8,256]{1,0:T(8,128)S(1)}, s32[8,128]{1,0:T(8,128)S(1)}) custom-call(s32[1]{0:T(128)} %bitcast.22.me_ref, s32[1024,1]{1,0:T(8,128)S(1)} %get-tuple-element.233.a_ref, s32[1024,1]{1,0:T(8,128)S(1)} %get-tuple-element.232.b_ref), custom_call_target="tpu_custom_call" | custom-call | flops 10000000 | bytes 1000000 | tf_op jit(solution)/shard_map/route/pallas_call | solution.py:214
  23.4 566.7 %conditional.1 = (f32[128,4096]{1,0:T(8,128)}) conditional(s32[]{:T(128)} %bitcast.24, (s32[256,4,2]{0,2,1:T(2,128)S(1)}, f32[128,4096]{1,0:T(8,128)S(1)}, s32[512,3]{0,1:T(4,128)S(1)}) %tuple.95, (s32[512,3]{0,1:T(4,128)S(1)}, f32[128,4096]{1,0:T(8,128)S(1)}, s32[8,256]{1,0:T(8,128)S(1)}, s32[8,128]{1,0:T(8,128)S(1)}, s32[]{:T(128)}) %tuple.96), branch_computations={%region_0.12_spmd, %region_12.13_spmd} | conditional | flops 125572864 | bytes 212146080 | solution.py:508
  33.9 17.7 %send0_1.1 = f32[32,32,128]{2,1,0:T(8,128)} custom-call(s32[8,256]{1,0:T(8,128)S(1)} %get-tuple-element.130.idx_ref.slot_ref, f32[128,32,128]{2,1,0:T(8,128)} %bitcast.72), custom_call_target="tpu_custom_call" | custom-call | bytes 1048576 | tf_op jit(solution)/shard_map/cond/branch_1_fun/send0_1/pallas_call | solution.py:253
  53.6 17.7 %send0_2.1 = f32[32,32,128]{2,1,0:T(8,128)} custom-call(s32[8,256]{1,0:T(8,128)S(1)} %get-tuple-element.130.idx_ref.slot_ref, f32[128,32,128]{2,1,0:T(8,128)} %bitcast.73), custom_call_target="tpu_custom_call" | custom-call | bytes 1048576 | tf_op jit(solution)/shard_map/cond/branch_1_fun/send0_2/pallas_call | solution.py:253
  73.8 17.7 %send0_3.1 = f32[32,32,128]{2,1,0:T(8,128)} custom-call(s32[8,256]{1,0:T(8,128)S(1)} %get-tuple-element.130.idx_ref.slot_ref, f32[128,32,128]{2,1,0:T(8,128)} %bitcast.74), custom_call_target="tpu_custom_call" | custom-call | bytes 1048576 | tf_op jit(solution)/shard_map/cond/branch_1_fun/send0_3/pallas_call | solution.py:253
  104.8 65.2 %deal0.1 = f32[128,32,128]{2,1,0:T(8,128)} custom-call(s32[8,128]{1,0:T(8,128)S(1)} %get-tuple-element.129.idx_ref.pos_ref, f32[128,32,128]{2,1,0:T(8,128)} %bitcast.75, f32[32,32,128]{2,1,0:T(8,128)} %copy-done.13, f32[32,32,128]{2,1,0:T(8,128)} %copy-done.15, f32[32,32,128]{2,1,0:T(8,128)} %copy-done.16), custom_call_target="tpu_custom_call" | custom-call | bytes 4194304 | tf_op jit(solution)/shard_map/cond/branch_1_fun/deal0/pallas_call | solution.py:253
  170.1 13.8 %all-to-all-start = ((f32[64,2,32,128]{3,2,1,0:T(8,128)}), f32[64,2,32,128]{3,2,1,0:T(8,128)S(1)}, u32[]{:S(2)}, u32[]{:S(2)}) async-start(f32[64,2,32,128]{3,2,1,0:T(8,128)} %bitcast.83), calls=%async_computation | async-start | bytes 4194304 | tf_op jit(solution)/shard_map/cond/branch_1_fun/all_to_all | solution.py:490
  183.9 17.7 %send1_1.1 = f32[32,32,128]{2,1,0:T(8,128)} custom-call(s32[8,256]{1,0:T(8,128)S(1)} %get-tuple-element.130.idx_ref.slot_ref, f32[128,32,128]{2,1,0:T(8,128)} %bitcast.76), custom_call_target="tpu_custom_call" | custom-call | bytes 1048576 | tf_op jit(solution)/shard_map/cond/branch_1_fun/send1_1/pallas_call | solution.py:253
  201.6 17.7 %send1_2.1 = f32[32,32,128]{2,1,0:T(8,128)} custom-call(s32[8,256]{1,0:T(8,128)S(1)} %get-tuple-element.130.idx_ref.slot_ref, f32[128,32,128]{2,1,0:T(8,128)} %bitcast.77), custom_call_target="tpu_custom_call" | custom-call | bytes 1048576 | tf_op jit(solution)/shard_map/cond/branch_1_fun/send1_2/pallas_call | solution.py:253
  222.9 17.7 %send1_3.1 = f32[32,32,128]{2,1,0:T(8,128)} custom-call(s32[8,256]{1,0:T(8,128)S(1)} %get-tuple-element.130.idx_ref.slot_ref, f32[128,32,128]{2,1,0:T(8,128)} %bitcast.78), custom_call_target="tpu_custom_call" | custom-call | bytes 1048576 | tf_op jit(solution)/shard_map/cond/branch_1_fun/send1_3/pallas_call | solution.py:253
  240.7 12.7 %collective-permute-done.8.refs_3_ = f32[32,32,128]{2,1,0:T(8,128)} collective-permute-done((f32[32,32,128]{2,1,0:T(8,128)}, f32[32,32,128]{2,1,0:T(8,128)}, u32[]{:S(2)}, u32[]{:S(2)}) %collective-permute-start.8) | collective-permute-done | bytes 524320 | tf_op jit(solution)/shard_map/cond/branch_1_fun/ppermute | solution.py:465
  253.4 65.2 %deal1.1 = f32[128,32,128]{2,1,0:T(8,128)} custom-call(s32[8,128]{1,0:T(8,128)S(1)} %get-tuple-element.129.idx_ref.pos_ref, f32[128,32,128]{2,1,0:T(8,128)} %bitcast.79, f32[32,32,128]{2,1,0:T(8,128)} %copy-done.12, f32[32,32,128]{2,1,0:T(8,128)} %copy-done.14, f32[32,32,128]{2,1,0:T(8,128)} %collective-permute-done.8.refs_3_), custom_call_target="tpu_custom_call" | custom-call | bytes 4194304 | tf_op jit(solution)/shard_map/cond/branch_1_fun/deal1/pallas_call | solution.py:253
  318.7 12.1 %all-to-all-start.2 = ((f32[64,2,32,128]{3,2,1,0:T(8,128)}), f32[64,2,32,128]{3,2,1,0:T(8,128)}, u32[]{:S(2)}, u32[]{:S(2)}) async-start(f32[64,2,32,128]{3,2,1,0:T(8,128)} %bitcast.84), calls=%async_computation.2 | async-start | bytes 4194304 | tf_op jit(solution)/shard_map/cond/branch_1_fun/all_to_all | solution.py:490
  331.1 17.8 %solve0.1 = f32[64,2,32,128]{3,2,1,0:T(8,128)S(1)} custom-call(s32[1]{0:T(128)} %bitcast.17.place_ref, s32[8,128]{1,0:T(8,128)S(1)} %get-tuple-element.129.idx_ref.pos_ref, s32[1536]{0:T(1024)S(1)} %reshape.246.anchor_ref, f32[64,2,32,128]{3,2,1,0:T(8,128)S(1)} %all-to-all-done.in_ref), custom_call_target="tpu_custom_call" | custom-call | flops 60000000 | bytes 30000000 | tf_op jit(solution)/shard_map/cond/branch_1_fun/solve0/pallas_call | solution.py:394
  350.3 31.6 %all-to-all-done.2.in_ref = f32[64,2,32,128]{3,2,1,0:T(8,128)} async-done(((f32[64,2,32,128]{3,2,1,0:T(8,128)}), f32[64,2,32,128]{3,2,1,0:T(8,128)}, u32[]{:S(2)}, u32[]{:S(2)}) %all-to-all-start.2) | async-done | bytes 2097184 | tf_op jit(solution)/shard_map/cond/branch_1_fun/all_to_all | solution.py:490
  387.8 18.7 %solve1.1 = f32[64,2,32,128]{3,2,1,0:T(8,128)S(1)} custom-call(s32[1]{0:T(128)} %bitcast.17.place_ref, s32[8,128]{1,0:T(8,128)S(1)} %get-tuple-element.129.idx_ref.pos_ref, s32[1536]{0:T(1024)S(1)} %reshape.246.anchor_ref, f32[64,2,32,128]{3,2,1,0:T(8,128)} %all-to-all-done.2.in_ref), custom_call_target="tpu_custom_call" | custom-call | flops 60000000 | bytes 30000000 | tf_op jit(solution)/shard_map/cond/branch_1_fun/solve1/pallas_call | solution.py:394
  407.8 31.2 %all-to-all-done.1.refs_0_ = f32[64,2,32,128]{3,2,1,0:T(8,128)S(1)} async-done(((f32[64,2,32,128]{3,2,1,0:T(8,128)}), f32[64,2,32,128]{3,2,1,0:T(8,128)S(1)}, u32[]{:S(2)}, u32[]{:S(2)}) %all-to-all-start.1) | async-done | bytes 2097184 | tf_op jit(solution)/shard_map/cond/branch_1_fun/all_to_all | solution.py:494
  446.3 17.7 %back0_1.1 = f32[32,32,128]{2,1,0:T(8,128)} custom-call(s32[8,256]{1,0:T(8,128)S(1)} %get-tuple-element.130.idx_ref.slot_ref, f32[128,32,128]{2,1,0:T(8,128)} %bitcast.69), custom_call_target="tpu_custom_call" | custom-call | bytes 1048576 | tf_op jit(solution)/shard_map/cond/branch_1_fun/back0_1/pallas_call | solution.py:253
  465.3 17.7 %back0_2.1 = f32[32,32,128]{2,1,0:T(8,128)} custom-call(s32[8,256]{1,0:T(8,128)S(1)} %get-tuple-element.130.idx_ref.slot_ref, f32[128,32,128]{2,1,0:T(8,128)} %bitcast.70), custom_call_target="tpu_custom_call" | custom-call | bytes 1048576 | tf_op jit(solution)/shard_map/cond/branch_1_fun/back0_2/pallas_call | solution.py:253
  483.0 17.7 %back0_3.1 = f32[32,32,128]{2,1,0:T(8,128)} custom-call(s32[8,256]{1,0:T(8,128)S(1)} %get-tuple-element.130.idx_ref.slot_ref, f32[128,32,128]{2,1,0:T(8,128)} %bitcast.71), custom_call_target="tpu_custom_call" | custom-call | bytes 1048576 | tf_op jit(solution)/shard_map/cond/branch_1_fun/back0_3/pallas_call | solution.py:253
  501.3 17.7 %back1_2.1 = f32[32,32,128]{2,1,0:T(8,128)} custom-call(s32[8,256]{1,0:T(8,128)S(1)} %get-tuple-element.130.idx_ref.slot_ref, f32[128,32,128]{2,1,0:T(8,128)} %bitcast.21.refs_0_), custom_call_target="tpu_custom_call" | custom-call | bytes 1048576 | tf_op jit(solution)/shard_map/cond/branch_1_fun/back1_2/pallas_call | solution.py:253
  519.0 17.7 %back1_3.1 = f32[32,32,128]{2,1,0:T(8,128)} custom-call(s32[8,256]{1,0:T(8,128)S(1)} %get-tuple-element.130.idx_ref.slot_ref, f32[128,32,128]{2,1,0:T(8,128)} %bitcast.21.refs_0_), custom_call_target="tpu_custom_call" | custom-call | bytes 1048576 | tf_op jit(solution)/shard_map/cond/branch_1_fun/back1_3/pallas_call | solution.py:253
  536.7 17.7 %back1_1.1 = f32[32,32,128]{2,1,0:T(8,128)} custom-call(s32[8,256]{1,0:T(8,128)S(1)} %get-tuple-element.130.idx_ref.slot_ref, f32[128,32,128]{2,1,0:T(8,128)} %bitcast.21.refs_0_), custom_call_target="tpu_custom_call" | custom-call | bytes 1048576 | tf_op jit(solution)/shard_map/cond/branch_1_fun/back1_1/pallas_call | solution.py:253
  568.9 12.7 %collective-permute-done.11 = f32[32,32,128]{2,1,0:T(8,128)S(1)} collective-permute-done((f32[32,32,128]{2,1,0:T(8,128)S(1)}, f32[32,32,128]{2,1,0:T(8,128)S(1)}, u32[]{:S(2)}, u32[]{:S(2)}) %collective-permute-start.11) | collective-permute-done | bytes 524320 | tf_op jit(solution)/shard_map/cond/branch_1_fun/ppermute | solution.py:465
  (66 shorter events, 68.1 us)
Async XLA Ops:
  6.5 16.9 %copy-start.17 = (s32[256,4,2]{0,2,1:T(2,128)S(1)}, s32[256,4,2]{0,2,1:T(2,128)}, u32[]{:S(2)}) copy-start(s32[256,4,2]{0,2,1:T(2,128)} %param.9) | copy-start | bytes 24580
  6.5 16.9 %copy-start.7 = (f32[128,4096]{1,0:T(8,128)S(1)}, f32[128,4096]{1,0:T(8,128)}, u32[]{:S(2)}) copy-start(f32[128,4096]{1,0:T(8,128)} %param.7) | copy-start | bytes 6291460
  6.5 16.9 %copy-start.18 = (s32[512,3]{0,1:T(4,128)S(1)}, s32[512,3]{0,1:T(4,128)}, u32[]{:S(2)}) copy-start(s32[512,3]{0,1:T(4,128)} %param.8) | copy-start | bytes 18436
  51.5 41.2 %collective-permute-start = (f32[32,32,128]{2,1,0:T(8,128)}, f32[32,32,128]{2,1,0:T(8,128)S(1)}, u32[]{:S(2)}, u32[]{:S(2)}) collective-permute-start(f32[32,32,128]{2,1,0:T(8,128)} %send0_1.1), channel_id=1, source_target_pairs={{0,64},{64,128},{128,192},{192,0},{1,65},{65,129},{129,193},{193,1... | collective-permute-start | bytes 1572872 | tf_op jit(solution)/shard_map/cond/branch_1_fun/ppermute | solution.py:465
  71.3 21.4 %collective-permute-start.1 = (f32[32,32,128]{2,1,0:T(8,128)}, f32[32,32,128]{2,1,0:T(8,128)S(1)}, u32[]{:S(2)}, u32[]{:S(2)}) collective-permute-start(f32[32,32,128]{2,1,0:T(8,128)} %send0_2.1), channel_id=1, source_target_pairs={{0,128},{64,192},{128,0},{192,64},{1,129},{65,193},{129,1},{193,65... | collective-permute-start | bytes 1572872 | tf_op jit(solution)/shard_map/cond/branch_1_fun/ppermute | solution.py:465
  91.5 12.5 %collective-permute-start.2 = (f32[32,32,128]{2,1,0:T(8,128)}, f32[32,32,128]{2,1,0:T(8,128)S(1)}, u32[]{:S(2)}, u32[]{:S(2)}) collective-permute-start(f32[32,32,128]{2,1,0:T(8,128)} %send0_3.1), channel_id=1, source_target_pairs={{0,192},{64,0},{128,64},{192,128},{1,193},{65,1},{129,65},{193,129... | collective-permute-start | bytes 1572872 | tf_op jit(solution)/shard_map/cond/branch_1_fun/ppermute | solution.py:465
  170.1 148.6 %all-to-all-start = ((f32[64,2,32,128]{3,2,1,0:T(8,128)}), f32[64,2,32,128]{3,2,1,0:T(8,128)S(1)}, u32[]{:S(2)}, u32[]{:S(2)}) async-start(f32[64,2,32,128]{3,2,1,0:T(8,128)} %bitcast.83), calls=%async_computation | async-start | bytes 4194304 | tf_op jit(solution)/shard_map/cond/branch_1_fun/all_to_all | solution.py:490
  201.5 39.1 %collective-permute-start.6 = (f32[32,32,128]{2,1,0:T(8,128)}, f32[32,32,128]{2,1,0:T(8,128)S(1)}, u32[]{:S(2)}, u32[]{:S(2)}) collective-permute-start(f32[32,32,128]{2,1,0:T(8,128)} %send1_1.1), channel_id=1, source_target_pairs={{0,64},{64,128},{128,192},{192,0},{1,65},{65,129},{129,193},{193,1... | collective-permute-start | bytes 1572872 | tf_op jit(solution)/shard_map/cond/branch_1_fun/ppermute | solution.py:465
  219.3 21.4 %collective-permute-start.7 = (f32[32,32,128]{2,1,0:T(8,128)}, f32[32,32,128]{2,1,0:T(8,128)S(1)}, u32[]{:S(2)}, u32[]{:S(2)}) collective-permute-start(f32[32,32,128]{2,1,0:T(8,128)} %send1_2.1), channel_id=1, source_target_pairs={{0,128},{64,192},{128,0},{192,64},{1,129},{65,193},{129,1},{193,65... | collective-permute-start | bytes 1572872 | tf_op jit(solution)/shard_map/cond/branch_1_fun/ppermute | solution.py:465
  240.6 12.8 %collective-permute-start.8 = (f32[32,32,128]{2,1,0:T(8,128)}, f32[32,32,128]{2,1,0:T(8,128)}, u32[]{:S(2)}, u32[]{:S(2)}) collective-permute-start(f32[32,32,128]{2,1,0:T(8,128)} %send1_3.1), channel_id=1, source_target_pairs={{0,192},{64,0},{128,64},{192,128},{1,193},{65,1},{129,65},{193,129... | collective-permute-start | bytes 1572872 | tf_op jit(solution)/shard_map/cond/branch_1_fun/ppermute | solution.py:465
  240.7 12.7 %copy-start.12 = (f32[32,32,128]{2,1,0:T(8,128)}, f32[32,32,128]{2,1,0:T(8,128)S(1)}, u32[]{:S(2)}) copy-start(f32[32,32,128]{2,1,0:T(8,128)S(1)} %collective-permute-done.6.refs_1_) | copy-start | bytes 1572868 | tf_op jit(solution)/shard_map/cond
  240.7 12.7 %copy-start.14 = (f32[32,32,128]{2,1,0:T(8,128)}, f32[32,32,128]{2,1,0:T(8,128)S(1)}, u32[]{:S(2)}) copy-start(f32[32,32,128]{2,1,0:T(8,128)S(1)} %collective-permute-done.7.refs_2_) | copy-start | bytes 1572868 | tf_op jit(solution)/shard_map/cond
  318.7 63.3 %all-to-all-start.2 = ((f32[64,2,32,128]{3,2,1,0:T(8,128)}), f32[64,2,32,128]{3,2,1,0:T(8,128)}, u32[]{:S(2)}, u32[]{:S(2)}) async-start(f32[64,2,32,128]{3,2,1,0:T(8,128)} %bitcast.84), calls=%async_computation.2 | async-start | bytes 4194304 | tf_op jit(solution)/shard_map/cond/branch_1_fun/all_to_all | solution.py:490
  381.9 57.1 %all-to-all-start.1 = ((f32[64,2,32,128]{3,2,1,0:T(8,128)}), f32[64,2,32,128]{3,2,1,0:T(8,128)S(1)}, u32[]{:S(2)}, u32[]{:S(2)}) async-start(f32[64,2,32,128]{3,2,1,0:T(8,128)} %copy-done.3), calls=%async_computation.1 | async-start | bytes 4194304 | tf_op jit(solution)/shard_map/cond/branch_1_fun/all_to_all | solution.py:494
  440.3 61.0 %all-to-all-start.3 = ((f32[64,2,32,128]{3,2,1,0:T(8,128)}), f32[64,2,32,128]{3,2,1,0:T(8,128)}, u32[]{:S(2)}, u32[]{:S(2)}) async-start(f32[64,2,32,128]{3,2,1,0:T(8,128)} %copy-done.2), calls=%async_computation.3 | async-start | bytes 4194304 | tf_op jit(solution)/shard_map/cond/branch_1_fun/all_to_all | solution.py:494
  464.0 94.0 %collective-permute-start.3 = (f32[32,32,128]{2,1,0:T(8,128)}, f32[32,32,128]{2,1,0:T(8,128)S(1)}, u32[]{:S(2)}, u32[]{:S(2)}) collective-permute-start(f32[32,32,128]{2,1,0:T(8,128)} %back0_1.1), channel_id=1, source_target_pairs={{0,192},{64,0},{128,64},{192,128},{1,193},{65,1},{129,65},{193,129... | collective-permute-start | bytes 1572872 | tf_op jit(solution)/shard_map/cond/branch_1_fun/ppermute | solution.py:465
  483.0 17.7 %copy-start.10 = (f32[32,32,128]{2,1,0:T(8,128)S(1)}, f32[32,32,128]{2,1,0:T(8,128)}, u32[]{:S(2)}) copy-start(f32[32,32,128]{2,1,0:T(8,128)} %back0_2.1) | copy-start | bytes 1572868 | tf_op jit(solution)/shard_map/cond
  500.7 60.0 %collective-permute-start.4 = (f32[32,32,128]{2,1,0:T(8,128)S(1)}, f32[32,32,128]{2,1,0:T(8,128)S(1)}, u32[]{:S(2)}, u32[]{:S(2)}) collective-permute-start(f32[32,32,128]{2,1,0:T(8,128)S(1)} %copy-done.10), channel_id=1, source_target_pairs={{0,128},{64,192},{128,0},{192,64},{1,129},{65,193},{129,1},{193,65... | collective-permute-start | bytes 1572872 | tf_op jit(solution)/shard_map/cond/branch_1_fun/ppermute | solution.py:465
  501.0 59.6 %collective-permute-start.5 = (f32[32,32,128]{2,1,0:T(8,128)}, f32[32,32,128]{2,1,0:T(8,128)}, u32[]{:S(2)}, u32[]{:S(2)}) collective-permute-start(f32[32,32,128]{2,1,0:T(8,128)} %back0_3.1), channel_id=1, source_target_pairs={{0,64},{64,128},{128,192},{192,0},{1,65},{65,129},{129,193},{193,1... | collective-permute-start | bytes 1572872 | tf_op jit(solution)/shard_map/cond/branch_1_fun/ppermute | solution.py:465
  519.0 35.4 %copy-start.11 = (f32[32,32,128]{2,1,0:T(8,128)S(1)}, f32[32,32,128]{2,1,0:T(8,128)}, u32[]{:S(2)}) copy-start(f32[32,32,128]{2,1,0:T(8,128)} %back1_2.1) | copy-start | bytes 1572868 | tf_op jit(solution)/shard_map/cond
  536.7 21.3 %copy-start.9 = (f32[32,32,128]{2,1,0:T(8,128)S(1)}, f32[32,32,128]{2,1,0:T(8,128)}, u32[]{:S(2)}) copy-start(f32[32,32,128]{2,1,0:T(8,128)} %back1_3.1) | copy-start | bytes 1572868 | tf_op jit(solution)/shard_map/cond
  554.4 14.5 %collective-permute-start.10 = (f32[32,32,128]{2,1,0:T(8,128)S(1)}, f32[32,32,128]{2,1,0:T(8,128)S(1)}, u32[]{:S(2)}, u32[]{:S(2)}) collective-permute-start(f32[32,32,128]{2,1,0:T(8,128)S(1)} %copy-done.11), channel_id=1, source_target_pairs={{0,128},{64,192},{128,0},{192,64},{1,129},{65,193},{129,1},{193,65... | collective-permute-start | bytes 1572872 | tf_op jit(solution)/shard_map/cond/branch_1_fun/ppermute | solution.py:465
  558.0 23.6 %collective-permute-start.11 = (f32[32,32,128]{2,1,0:T(8,128)S(1)}, f32[32,32,128]{2,1,0:T(8,128)S(1)}, u32[]{:S(2)}, u32[]{:S(2)}) collective-permute-start(f32[32,32,128]{2,1,0:T(8,128)S(1)} %copy-done.9), channel_id=1, source_target_pairs={{0,64},{64,128},{128,192},{192,0},{1,65},{65,129},{129,193},{193,1... | collective-permute-start | bytes 1572872 | tf_op jit(solution)/shard_map/cond/branch_1_fun/ppermute | solution.py:465
  558.0 23.6 %collective-permute-start.9 = (f32[32,32,128]{2,1,0:T(8,128)}, f32[32,32,128]{2,1,0:T(8,128)S(1)}, u32[]{:S(2)}, u32[]{:S(2)}) collective-permute-start(f32[32,32,128]{2,1,0:T(8,128)} %back1_1.1), channel_id=1, source_target_pairs={{0,192},{64,0},{128,64},{192,128},{1,193},{65,1},{129,65},{193,129... | collective-permute-start | bytes 1572872 | tf_op jit(solution)/shard_map/cond/branch_1_fun/ppermute | solution.py:465
  (7 other events, 34.7 us)
